TPU v7x, 256 devices: a whole 4x4x8 slice. The times are simulated.
256 devices in a mesh: section: 4 (over x), dp: 16 (over z, core), mp: 4 (over y).
Axes of the slice: x: 4, y: 4, z: 8, core: 2. Of those that a mesh axis runs over, the one named last changes fastest.
Arguments:
- teacher_feats: bfloat16 [8, 2048, 8192], P('section', 'dp', 'mp')
- layer_map: int32 [4], replicated, may hold values from 0 to 7
- student_in: bfloat16 [4, 2048, 2048], P('section', 'dp', 'mp')
- layer_weight: bfloat16 [4, 2048, 2048], P('section', 'dp', 'mp'), may hold values from -0.125 to 0.125
- proj_weight: bfloat16 [4, 2048, 8192], P('section', None, 'mp'), may hold values from -0.0625 to 0.0625
- token_weight: float32 [2048], P('dp'), may hold values from 256 to 2048
Outputs:
- grad_inputs: bfloat16 [4, 2048, 2048], P('section', 'dp', 'mp')
- grad_layer: float32 [4, 2048, 2048], P('section', 'dp', 'mp')
- grad_proj: float32 [4, 2048, 8192], P('section', 'dp', 'mp')
All inputs are finite; a program needn't handle non-finite values.
Results may differ from a plain program's by a relative error of at most 0.023.
Values may be sent and summed in bfloat16 or wider, within the bound.
No kernel may reach another device: no remote copies, remote signals or barrier semaphores. Data moves between devices by JAX's collectives and lax.ppermute only.
A program may use at most 128 MiB of HBM per device.

v0:
```python
import jax
import jax.numpy as jnp
from jax import lax
from jax.sharding import PartitionSpec as P

epsilon_sq = 1e-06


def from_behind(array, axis, by):
    devices = lax.axis_size(axis)
    pairs = [(i, i + by) for i in range(devices) if 0 <= i + by < devices]
    return lax.ppermute(array, axis, pairs)


def on_device(teacher_feats, layer_map, student_in, layer_weight, proj_weight, token_weight):
    section_count = lax.axis_size("section")
    here = lax.axis_index("section")
    positions = jnp.arange(layer_map.shape[0], dtype=jnp.int32)
    target = jnp.sum(jnp.where(positions == here, layer_map, 0))
    piece = lax.all_gather(teacher_feats, "section", axis=0, tiled=True)
    layer_ids = jnp.arange(piece.shape[0], dtype=jnp.int32)
    onehot = (layer_ids == target).astype(jnp.bfloat16)
    picked = jnp.einsum("l,ltk->tk", onehot, piece, preferred_element_type=jnp.float32).astype(
        jnp.bfloat16
    )
    hidden = student_in[0]
    weight_part = layer_weight[0]
    project = proj_weight[0]
    full_hidden = lax.all_gather(hidden, "mp", axis=1, tiled=True)
    weight_cols = lax.all_gather(weight_part, "dp", axis=0, tiled=True)
    partial_value = jnp.einsum("te,ke->tk", picked, project, preferred_element_type=jnp.float32)
    proj = lax.psum_scatter(partial_value, "mp", scatter_dimension=1, tiled=True)
    pre = jnp.dot(full_hidden, weight_cols, preferred_element_type=jnp.float32)
    squash = jnp.tanh(pre)
    act = hidden.astype(jnp.float32) + squash
    slope = 1.0 - squash * squash
    sum_aa, sum_qq, sum_aq = lax.psum(
        (jnp.sum(act * act, axis=1), jnp.sum(proj * proj, axis=1), jnp.sum(act * proj, axis=1)),
        "mp",
    )
    inv_a = lax.rsqrt(sum_aa + epsilon_sq)
    inv_q = lax.rsqrt(sum_qq + epsilon_sq)
    cgrad = (-(token_weight * inv_a * inv_q))[:, None] * proj + (
        token_weight * sum_aq * inv_a**3 * inv_q
    )[:, None] * act
    qgrad = (
        (-(token_weight * inv_a * inv_q))[:, None] * act
        + (token_weight * sum_aq * inv_a * inv_q**3)[:, None] * proj
    ).astype(jnp.bfloat16)
    qgrad_full = lax.all_gather(qgrad, "mp", axis=1, tiled=True)
    incoming = jnp.zeros(cgrad.shape, jnp.float32)
    result = incoming
    sgate = jnp.zeros(cgrad.shape, jnp.bfloat16)
    for step in range(section_count):
        total = cgrad + incoming
        sgate = (total * slope).astype(jnp.bfloat16)
        spread = jnp.einsum("tn,kn->tk", sgate, weight_cols, preferred_element_type=jnp.float32)
        result = total + lax.psum_scatter(spread, "mp", scatter_dimension=1, tiled=True)
        if step + 1 < section_count:
            incoming = from_behind(result, "section", -1)
    rows = full_hidden
    grad_layer = lax.psum_scatter(
        jnp.einsum("tk,tn->kn", rows, sgate, preferred_element_type=jnp.float32).astype(
            jnp.bfloat16
        ),
        "dp",
        scatter_dimension=0,
        tiled=True,
    ).astype(jnp.float32)
    rows = qgrad_full
    grad_proj = lax.psum_scatter(
        jnp.einsum("tk,te->ke", rows, picked, preferred_element_type=jnp.float32).astype(
            jnp.bfloat16
        ),
        "dp",
        scatter_dimension=0,
        tiled=True,
    ).astype(jnp.float32)
    return (result.astype(jnp.bfloat16)[None], grad_layer[None], grad_proj[None])


def solution(mesh):
    placed = (
        P("section", "dp", "mp"),
        P(),
        P("section", "dp", "mp"),
        P("section", "dp", "mp"),
        P("section", None, "mp"),
        P("dp"),
    )
    return jax.shard_map(
        on_device,
        mesh=mesh,
        in_specs=placed,
        out_specs=(P("section", "dp", "mp"), P("section", "dp", "mp"), P("section", "dp", "mp")),
        check_vma=False,
    )
```

profile of v0, /device:TPU:6, one launch (start us, length us, event | category | flops | bytes accessed | tf_op | source)
XLA Modules:
  0.0 427.3 jit_solution(13894099906977529612)
XLA Ops:
  7.2 0.7 all-gather.5.cloned.1.call-update
  7.9 0.7 all-gather.7.cloned.1.call-update
  8.7 1.3 fusion.29
  10.0 51.8 %all-gather.5.cloned.1.call-done = bf16[8,128,2048]{2,1,0:T(8,128)(2,1)} async-done(((bf16[2,128,2048]{2,1,0:T(8,128)(2,1)}), bf16[8,128,2048]{2,1,0:T(8,128)(2,1)}) %all-gather.5.cloned.1.call-update) | async-done | bytes 4194320 | tf_op jit(solution)/shard_map/all_gather | solution.py:20
  61.8 5.9 %fusion.2 = bf16[1,128,2048]{2,0,1:T(2,128)(2,1)S(1)} fusion(bf16[8,128,2048]{2,1,0:T(8,128)(2,1)} %all-gather.5.cloned.1.call-done, s32[]{:T(128)} %fusion.29), kind=kOutput, calls=%fused_computation.3 | convolution fusion | flops 4194312 | bytes 4718596 | tf_op jit(solution)/shard_map/l,ltk->tk/dot_general | solution.py:23
  67.7 1.0 copy-done.1
  68.7 7.3 %fusion = f32[128,2048]{1,0:T(8,128)} fusion(bf16[1,2048,2048]{2,1,0:T(8,128)(2,1)} %param.10, bf16[1,128,2048]{2,0,1:T(2,128)(2,1)S(1)} %fusion.2), kind=kOutput, calls=%fused_computation | convolution fusion | flops 1073741824 | bytes 9961472 | tf_op jit(solution)/shard_map/te,ke->tk/dot_general | solution.py:31
  76.1 0.0 reduce-scatter.12.cloned.1.call-start
  76.1 13.4 %all-gather = bf16[1,128,2048]{2,1,0:T(8,128)(2,1)S(1)} all-gather(bf16[1,128,512]{2,1,0:T(8,128)(2,1)S(1)} %copy-done.3), channel_id=2, replica_groups=mesh['section'=4,'dp'=16,'mp'=4] {'mp'}, dimensions={2}, use_global_device_ids=true | all-gather | bytes 655360 | tf_op jit(solution)/shard_map/all_gather | solution.py:29
  89.5 15.8 %all-gather.7.cloned.1.call-done = bf16[1,2048,512]{2,1,0:T(8,128)(2,1)} async-done(((bf16[1,128,512]{2,1,0:T(8,128)(2,1)}), bf16[1,2048,512]{2,1,0:T(8,128)(2,1)}) %all-gather.7.cloned.1.call-update) | async-done | bytes 2097168 | tf_op jit(solution)/shard_map/all_gather | solution.py:30
  105.3 27.8 %reduce-scatter.10.cloned.1.call-done = f32[128,512]{1,0:T(8,128)} async-done(((f32[128,2048]{1,0:T(8,128)}), f32[128,512]{1,0:T(8,128)}) %reduce-scatter.10.cloned.1.call-update) | async-done | bytes 262160 | tf_op jit(solution)/shard_map/reduce_scatter | solution.py:32
  133.1 2.2 multiply_reduce_fusion.2
  135.3 8.4 %all-reduce = (f32[128]{0:T(128)S(1)}, f32[128]{0:T(128)S(1)}, f32[128]{0:T(128)S(1)}) all-reduce(f32[128]{0:T(128)S(1)} %get-tuple-element.10, f32[128]{0:T(128)S(1)} %get-tuple-element.9, f32[128]{0:T(128)S(1)} %get-tuple-element.11), channel_id=1, replica_groups=mesh['section'=4,'dp'=16,'mp'=4] {'mp'}, use_global_device_ids=true, to_apply=%region_7.8 | all-reduce | flops 384 | bytes 3072 | tf_op jit(solution)/shard_map/psum | solution.py:37
  143.8 0.8 add_convert_fusion
  144.6 1.8 fusion.11
  146.4 0.0 reduce-scatter.14.cloned.1.call-start
  146.4 25.8 %reduce-scatter.12.cloned.1.call-done = f32[128,512]{1,0:T(8,128)} async-done(((f32[128,2048]{1,0:T(8,128)}), f32[128,512]{1,0:T(8,128)}) %reduce-scatter.12.cloned.1.call-update) | async-done | bytes 262160 | tf_op jit(solution)/shard_map/reduce_scatter | solution.py:58
  172.3 1.0 add.60
  173.3 2.8 collective-permute-start
  176.0 3.9 collective-permute-done
  179.9 1.8 fusion.9
  181.8 0.0 reduce-scatter.16.cloned.1.call-start
  181.8 27.9 %reduce-scatter.14.cloned.1.call-done = f32[128,512]{1,0:T(8,128)} async-done(((f32[128,2048]{1,0:T(8,128)}), f32[128,512]{1,0:T(8,128)}) %reduce-scatter.14.cloned.1.call-update) | async-done | bytes 262160 | tf_op jit(solution)/shard_map/reduce_scatter | solution.py:58
  209.7 1.0 add.62
  210.7 2.9 collective-permute-start.1
  213.6 4.1 collective-permute-done.1
  217.7 1.8 fusion.7
  219.5 0.0 reduce-scatter.18.cloned.1.call-start
  219.6 27.6 %reduce-scatter.16.cloned.1.call-done = f32[128,512]{1,0:T(8,128)} async-done(((f32[128,2048]{1,0:T(8,128)}), f32[128,512]{1,0:T(8,128)}) %reduce-scatter.16.cloned.1.call-update) | async-done | bytes 262160 | tf_op jit(solution)/shard_map/reduce_scatter | solution.py:58
  247.1 1.0 add.64
  248.1 2.8 collective-permute-start.2
  250.9 3.9 collective-permute-done.2
  254.8 0.1 multiply_convert_fusion
  254.9 1.8 fusion.5
  256.7 0.0 reduce-scatter.22.cloned.1.call-start
  256.7 0.7 fusion.4
  257.5 2.6 copy.13
  260.0 0.0 reduce-scatter.20.cloned.1.call-start
  260.1 0.8 copy-done.5
  260.9 14.2 %all_gather.15 = bf16[128,2048]{1,0:T(8,128)(2,1)S(1)} all-gather(bf16[128,512]{1,0:T(8,128)(2,1)S(1)} %copy-done.5), channel_id=1, replica_groups=mesh['section'=4,'dp'=16,'mp'=4] {'mp'}, dimensions={1}, use_global_device_ids=true | all-gather | bytes 655360 | tf_op jit(solution)/shard_map/all_gather | solution.py:50
  275.1 5.6 %convolution_convert_fusion = bf16[2048,2048]{1,0:T(8,128)(2,1)} fusion(bf16[128,2048]{1,0:T(8,128)(2,1)S(1)} %all_gather.15, bf16[1,128,2048]{2,0,1:T(2,128)(2,1)S(1)} %copy-done.2), kind=kOutput, calls=%fused_computation.2 | convolution fusion | flops 1077936128 | bytes 9437184 | tf_op jit(solution)/shard_map/tk,te->ke/dot_general | solution.py:72
  280.7 4.3 %reduce-scatter.18.cloned.1.call-done = f32[128,512]{1,0:T(8,128)} async-done(((f32[128,2048]{1,0:T(8,128)}), f32[128,512]{1,0:T(8,128)}) %reduce-scatter.18.cloned.1.call-update) | async-done | bytes 262160 | tf_op jit(solution)/shard_map/reduce_scatter | solution.py:58
  285.1 1.6 fusion.20
  286.7 60.0 %reduce-scatter.22.cloned.1.call-done = bf16[128,512]{1,0:T(8,128)(2,1)} async-done(((bf16[2048,512]{1,0:T(8,128)(2,1)}), bf16[128,512]{1,0:T(8,128)(2,1)}) %reduce-scatter.22.cloned.1.call-update) | async-done | bytes 131088
  346.7 1.0 copy.14
  347.8 0.8 copy.10
  348.6 70.0 %reduce-scatter.20.cloned.1.call-done = bf16[128,2048]{1,0:T(8,128)(2,1)} async-done(((bf16[2048,2048]{1,0:T(8,128)(2,1)}), bf16[128,2048]{1,0:T(8,128)(2,1)}) %reduce-scatter.20.cloned.1.call-update) | async-done | bytes 524304 | tf_op jit(solution)/shard_map/reduce_scatter | solution.py:71
  418.6 2.1 bitcast_convert_fusion.1
  (26 shorter events, 0.4 us)
Async XLA Ops:
  7.2 54.6 %all-gather.5.cloned.1.call-start = ((), (), s32[]{:S(2)}) async-start(), calls=%async_computation.7 | async-start | bytes 5242880 | tf_op jit(solution)/shard_map/all_gather | solution.py:20
  7.9 97.4 %all-gather.7.cloned.1.call-start = ((), (), s32[]{:S(2)}) async-start(), calls=%async_computation.14 | async-start | bytes 2228224 | tf_op jit(solution)/shard_map/all_gather | solution.py:30
  8.6 124.4 %reduce-scatter.10.cloned.1.call-start = ((), (), s32[]{:S(2)}) async-start(), calls=%async_computation.8 | async-start | bytes 1310720 | tf_op jit(solution)/shard_map/reduce_scatter | solution.py:32
  67.7 1.0 copy-start.1
  68.7 7.4 %copy-start.3 = (bf16[1,128,512]{2,1,0:T(8,128)(2,1)S(1)}, bf16[1,128,512]{2,1,0:T(8,128)(2,1)}, u32[]{:S(2)}) copy-start(bf16[1,128,512]{2,1,0:T(8,128)(2,1)} %param.8) | copy-start | bytes 393220
  76.1 67.7 %copy-start.6 = (f32[128]{0:T(128)S(1)}, f32[128]{0:T(128)}, u32[]{:S(2)}) copy-start(f32[128]{0:T(128)} %param.11) | copy-start | bytes 1540
  76.1 96.2 %reduce-scatter.12.cloned.1.call-start = ((), (), s32[]{:S(2)}) async-start(), calls=%async_computation.9 | async-start | bytes 1310720 | tf_op jit(solution)/shard_map/reduce_scatter | solution.py:58
  105.3 39.3 %copy-start = (bf16[1,2048,512]{2,1,0:T(8,128)(2,1)S(1)}, bf16[1,2048,512]{2,1,0:T(8,128)(2,1)}, u32[]{:S(2)}) copy-start(bf16[1,2048,512]{2,1,0:T(8,128)(2,1)} %all-gather.7.cloned.1.call-done) | copy-start | bytes 6291460
  133.1 10.7 %copy-start.4 = (f32[128,512]{1,0:T(8,128)S(1)}, f32[128,512]{1,0:T(8,128)}, u32[]{:S(2)}) copy-start(f32[128,512]{1,0:T(8,128)} %reduce-scatter.10.cloned.1.call-done) | copy-start | bytes 786436
  146.4 63.3 %reduce-scatter.14.cloned.1.call-start = ((), (), s32[]{:S(2)}) async-start(), calls=%async_computation.10 | async-start | bytes 1310720 | tf_op jit(solution)/shard_map/reduce_scatter | solution.py:58
  173.3 6.6 %collective-permute-start = (f32[128,512]{1,0:T(8,128)S(1)}, f32[128,512]{1,0:T(8,128)S(1)}, u32[]{:S(2)}, u32[]{:S(2)}) collective-permute-start(f32[128,512]{1,0:T(8,128)S(1)} %add.60), channel_id=1, source_target_pairs={{64,0},{128,64},{192,128},{65,1},{129,65},{193,129},{66,2},{130,66... | collective-permute-start | bytes 786440 | tf_op jit(solution)/shard_map/ppermute | solution.py:12
  181.8 65.4 %reduce-scatter.16.cloned.1.call-start = ((), (), s32[]{:S(2)}) async-start(), calls=%async_computation.11 | async-start | bytes 1310720 | tf_op jit(solution)/shard_map/reduce_scatter | solution.py:58
  210.7 7.0 %collective-permute-start.1 = (f32[128,512]{1,0:T(8,128)S(1)}, f32[128,512]{1,0:T(8,128)S(1)}, u32[]{:S(2)}, u32[]{:S(2)}) collective-permute-start(f32[128,512]{1,0:T(8,128)S(1)} %add.62), channel_id=1, source_target_pairs={{64,0},{128,64},{192,128},{65,1},{129,65},{193,129},{66,2},{130,66... | collective-permute-start | bytes 786440 | tf_op jit(solution)/shard_map/ppermute | solution.py:12
  219.5 65.6 %reduce-scatter.18.cloned.1.call-start = ((), (), s32[]{:S(2)}) async-start(), calls=%async_computation.12 | async-start | bytes 1310720 | tf_op jit(solution)/shard_map/reduce_scatter | solution.py:58
  248.1 6.7 %collective-permute-start.2 = (f32[128,512]{1,0:T(8,128)S(1)}, f32[128,512]{1,0:T(8,128)S(1)}, u32[]{:S(2)}, u32[]{:S(2)}) collective-permute-start(f32[128,512]{1,0:T(8,128)S(1)} %add.64), channel_id=1, source_target_pairs={{64,0},{128,64},{192,128},{65,1},{129,65},{193,129},{66,2},{130,66... | collective-permute-start | bytes 786440 | tf_op jit(solution)/shard_map/ppermute | solution.py:12
  256.7 90.0 %reduce-scatter.22.cloned.1.call-start = ((), (), s32[]{:S(2)}) async-start(), calls=%async_computation.15 | async-start | bytes 2228224
  260.0 0.9 copy-start.5
  260.0 15.1 %copy-start.2 = (bf16[1,128,2048]{2,0,1:T(2,128)(2,1)S(1)}, bf16[1,128,2048]{2,0,1:T(2,128)(2,1)}, u32[]{:S(2)}) copy-start(bf16[1,128,2048]{2,0,1:T(2,128)(2,1)} %copy-done.1) | copy-start | bytes 1572868
  260.0 158.6 %reduce-scatter.20.cloned.1.call-start = ((), (), s32[]{:S(2)}) async-start(), calls=%async_computation.13 | async-start | bytes 8912896 | tf_op jit(solution)/shard_map/reduce_scatter | solution.py:71
Sparse Core Ops, SparseCore 0:
  9.8 51.9 all-gather.4
  63.6 41.6 all-gather.6
  108.4 24.6 reduce-scatter.9
  146.5 25.7 reduce-scatter.11
  181.9 27.7 reduce-scatter.13
  219.6 27.4 reduce-scatter.15
  256.8 28.2 reduce-scatter.17
  287.8 58.8 reduce-scatter.21
  349.4 69.1 reduce-scatter.19
where the time goes:
time: 428 us; the launch traced here: 427 us
  waiting for transfers between devices  324 us (76%)
  blocking collectives  36 us (8%)
  matrix products  29 us (7%)
  between operations  14 us (3%)
  other arithmetic  8.99 us (2%)
  starting transfers between devices  8.84 us (2%)
  local copies, waits for them, and re-layouts  6.25 us (1%)
    reduce_scatter x4, waiting for transfers between devices, on_device(): lax.psum_scatter(spread, 'mp', scatter_dimension=1, tiled=True)  85.6 us
    reduce_scatter x1, waiting for transfers between devices, on_device(): lax.psum_scatter(jnp.einsum('tk,te->ke', rows, picked, preferred_element_...  70 us
    unnamed x10, waiting for transfers between devices  61.5 us
    all_gather x1, waiting for transfers between devices, on_device(): piece = lax.all_gather(teacher_feats, 'section', axis=0, tiled=True)  51.8 us
    reduce_scatter x1, waiting for transfers between devices, on_device(): lax.psum_scatter(partial_value, 'mp', scatter_dimension=1, tiled=True)  27.8 us
    all_gather x1, waiting for transfers between devices, on_device(): weight_cols = lax.all_gather(weight_part, 'dp', axis=0, tiled=True)  15.8 us
    all_gather x1, blocking collectives, on_device(): qgrad_full = lax.all_gather(qgrad, 'mp', axis=1, tiled=True)  14.2 us
    all_gather x1, blocking collectives, on_device(): full_hidden = lax.all_gather(hidden, 'mp', axis=1, tiled=True)  13.4 us
  transfers between devices with their start and end apart: 12, of which 12 were waited for; matrix products, arithmetic and copies ran while one was open for 6% of the time, Pallas kernels for 0%

commit v1 on v0

v1 whole, which is shorter than its diff:
```python
import jax
import jax.numpy as jnp
from jax import lax
from jax.experimental import pallas as pl
from jax.experimental.pallas import tpu as pltpu
from jax.sharding import PartitionSpec as P

epsilon_sq = 1e-06
bf16 = jnp.bfloat16
f32 = jnp.float32
TOK = 128
WIDE = 512


def shift(array, axis, by):
    n = lax.axis_size(axis)
    return lax.ppermute(array, axis, [(i, (i + by) % n) for i in range(n)])


def to_previous(array):
    n = lax.axis_size("section")
    return lax.ppermute(array, "section", [(i, i - 1) for i in range(1, n)])


def along_z():
    return [list(range(core, lax.axis_size("dp"), 2)) for core in (0, 1)]


def gather_z(array):
    return lax.all_gather(array, "dp", axis=0, axis_index_groups=along_z())


def sum_z(array):
    return lax.psum_scatter(array, "dp", scatter_dimension=0, tiled=True, axis_index_groups=along_z())


def cross(array, bits):
    n = lax.axis_size("dp")
    return lax.ppermute(array, "dp", [(i, i ^ bits) for i in range(n)])


def to_pair(array, by):
    n = lax.axis_size("dp")
    return lax.ppermute(array, "dp", [(i, (i + 4 * by) % n) for i in range(n)])


def after(array, *earlier):
    return lax.optimization_barrier((array,) + earlier)[0]


def call(body, outs, *args, scratch=(), flops=0, limit=12):
    scalars = pl.BlockSpec(memory_space=pltpu.SMEM)
    size = sum(a.size * a.dtype.itemsize for a in args)
    return pl.pallas_call(
        body,
        out_shape=[jax.ShapeDtypeStruct(shape, dtype) for shape, dtype in outs],
        in_specs=[scalars if a.dtype == jnp.int32 else pl.BlockSpec() for a in args],
        out_specs=[pl.BlockSpec()] * len(outs),
        scratch_shapes=list(scratch),
        compiler_params=pltpu.CompilerParams(vmem_limit_bytes=limit * 2**20),
        cost_estimate=pl.CostEstimate(flops=flops, bytes_accessed=size, transcendentals=0),
    )(*args)


def dot(a, b, over):
    return lax.dot_general(a, b, (((over[0],), (over[1],)), ((), ())), preferred_element_type=f32)


def places():
    m = lax.axis_index("mp")
    dp = lax.axis_index("dp")
    return m, dp // 4, dp % 4, dp // 2, dp % 2


def pre_body(h0, h1, h2, h3, mine, theirs, weight, act, slope):
    m, _, _, _, core = places()
    total = None
    for d, hidden in enumerate((h0, h1, h2, h3)):
        for i in range(4):
            r = 2 * lax.rem(m + d, 4) + i // 2

            @pl.when(core == i % 2)
            def _():
                weight[d, i * TOK : (i + 1) * TOK] = mine[r]

            @pl.when(core != i % 2)
            def _():
                weight[d, i * TOK : (i + 1) * TOK] = theirs[r]

        part = dot(hidden[...], weight[d], (1, 0))
        total = part if total is None else total + part
    squash = jnp.tanh(total)
    act[...] = h0[...].astype(f32) + squash
    slope[...] = 1.0 - squash * squash


def sums_body(own, c2, c1, c3, act, proj, sums):
    value = own[...] + c2[...].astype(f32) + c1[...].astype(f32) + c3[...].astype(f32)
    proj[...] = value
    side = act[...]
    lane = lax.broadcasted_iota(jnp.int32, (TOK, TOK), 1)
    columns = jnp.zeros((TOK, TOK), f32)
    for i, product in enumerate((side * side, value * value, side * value)):
        columns = jnp.where(lane == i, jnp.sum(product, axis=1, keepdims=True), columns)
    sums[...] = columns.T[:8]


def first_body(s0, s1, s2, s3, scale, act, proj, slope, weight, cgrad, qgrad, own, gate, p2, p1, p3):
    sums = s0[...] + s1[...] + s2[...] + s3[...]
    rows = jnp.concatenate([sums, jnp.broadcast_to(scale[...], (8, TOK)), jnp.zeros((TOK - 16, TOK), f32)], axis=0)
    columns = rows.T
    sum_aa, sum_qq, sum_aq, scales = columns[:, 0:1], columns[:, 1:2], columns[:, 2:3], columns[:, 8:9]
    inv_a = lax.rsqrt(sum_aa + epsilon_sq)
    inv_q = lax.rsqrt(sum_qq + epsilon_sq)
    both = -(scales * inv_a * inv_q)
    total = both * proj[...] + (scales * sum_aq * inv_a * inv_a * inv_a * inv_q) * act[...]
    cgrad[...] = total
    qgrad[...] = (both * act[...] + (scales * sum_aq * inv_a * inv_q * inv_q * inv_q) * proj[...]).astype(bf16)
    spread(total, slope, weight, own, gate, p2, p1, p3)


def step_body(incoming, cgrad, slope, weight, own, gate, p2, p1, p3):
    spread(cgrad[...] + incoming[...].astype(f32), slope, weight, own, gate, p2, p1, p3)


def spread(total, slope, weight, own, gate, p2, p1, p3):
    sgate = (total * slope[...]).astype(bf16)
    gate[...] = sgate
    for d, part in ((2, p2), (1, p1), (3, p3)):
        part[...] = dot(sgate, weight[d], (1, 1)).astype(bf16)
    own[...] = total + dot(sgate, weight[0], (1, 1))


def saved_body(h0, h1, h2, h3, s0, s1, s2, s3, held):
    m, pair, place, _, _ = places()
    for d, hidden in enumerate((h0, h1, h2, h3)):
        held[d] = hidden[...]
    for x, out in enumerate((s0, s1, s2, s3)):
        start = pl.multiple_of((place ^ x) * TOK, TOK)
        for by in range(4):
            d = lax.rem(pair + by - m + 4, 4)
            out[:, by * TOK : (by + 1) * TOK] = held[d, :, pl.ds(start, TOK)]


def split_body(q0, q1, q2, q3, keep, give, held):
    m, _, _, _, core = places()
    for d, value in enumerate((q0, q1, q2, q3)):
        held[d] = value[...]
    for chip in range(8):
        d = lax.rem(chip // 2 - m + 4, 4)
        for out, place in ((keep, core), (give, 1 - core)):
            start = pl.multiple_of(chip % 2 * 256 + place * TOK, TOK)
            out[:, chip * TOK : (chip + 1) * TOK] = held[d, :, pl.ds(start, TOK)]


def proj_grad_body(keep, came, picked, other, out):
    left = jnp.concatenate([keep[...], came[...]], axis=0)
    for tile in range(8):
        cut = slice(tile * 256, (tile + 1) * 256)
        right = jnp.concatenate([picked[:, cut], other[:, cut]], axis=0)
        out[:, cut] = dot(left, right, (0, 0)).astype(bf16)


def layer_grad_body(g0, g1, g2, g3, s0, s1, s2, s3, own, p1, p2, p3):
    gates = jnp.concatenate([g0[...], g1[...], g2[...], g3[...]], axis=0)
    for by, out in ((2, p2), (1, p1), (3, p3), (0, own)):
        cut = slice(by * TOK, (by + 1) * TOK)
        left = jnp.concatenate([s0[:, cut], s1[:, cut], s2[:, cut], s3[:, cut]], axis=0)
        out[...] = dot(left, gates, (0, 0)).astype(out.dtype)


def choose_body(layers, feats, across_first, across_last, own):
    here = lax.axis_index("section")
    half = TOK // 2
    far = feats.at[lax.rem(layers[lax.rem(here + 2, 4)], 2)]
    across_first[...] = far[:half]
    across_last[...] = far[half:]
    own[...] = feats[lax.rem(layers[here], 2)]


def merge_body(layers, feats, from_left, from_right, to_next, to_back):
    here = lax.axis_index("section")
    half = TOK // 2
    for out, target, came, through in (
        (to_next, lax.rem(here + 1, 4), from_left, slice(0, half)),
        (to_back, lax.rem(here + 3, 4), from_right, slice(half, TOK)),
    ):
        layer = layers[target]
        out[...] = feats[lax.rem(layer, 2)]

        @pl.when(lax.div(layer, 2) != here)
        def _():
            out[through] = came[...]


def picked_body(layers, own, left, right, out):
    here = lax.axis_index("section")
    half = TOK // 2
    gap = lax.rem(lax.div(layers[here], 2) - here + 4, 4)

    @pl.when(gap == 0)
    def _():
        out[...] = own[...]

    @pl.when(gap == 1)
    def _():
        out[...] = right[...]

    @pl.when(gap == 2)
    def _():
        out[:half] = left[:half]
        out[half:] = right[half:]

    @pl.when(gap == 3)
    def _():
        out[...] = left[...]


def on_device(teacher_feats, layer_map, student_in, layer_weight, proj_weight, token_weight):
    section_count = lax.axis_size("section")
    m = lax.axis_index("mp")
    hidden = student_in[0]
    block = ((TOK, WIDE), bf16)
    wide = ((TOK, WIDE), f32)
    held = [pltpu.VMEM((4, TOK, WIDE), bf16)]

    half = ((TOK // 2, 2048), bf16)
    rows = ((TOK, 2048), bf16)
    mine = gather_z(layer_weight[0])
    across_first, across_last, own = call(choose_body, [half, half, rows], layer_map, teacher_feats)
    from_left = shift(across_first, "section", 1)
    from_right = shift(across_last, "section", -1)
    to_next, to_back = call(merge_body, [rows, rows], layer_map, teacher_feats, from_left, from_right)
    left = shift(to_next, "section", 1)
    right = shift(to_back, "section", -1)
    start = after(hidden, to_next)
    hiddens = [hidden] + [shift(start, "mp", -d) for d in (1, 2, 3)]
    saved = call(saved_body, [block] * 4, *hiddens, scratch=held)
    (picked,) = call(picked_body, [rows], layer_map, after(own, *hiddens), left, right)

    project = proj_weight[0].reshape(4, WIDE, -1)
    partial = []
    for d in (2, 1, 3, 0):
        part = lax.dynamic_index_in_dim(project, (m + d) % 4, 0, keepdims=False)
        partial.append(jnp.einsum("te,ke->tk", picked, part, preferred_element_type=f32))
    own = partial[3]
    came = [shift(part.astype(bf16), "mp", d) for part, d in zip(partial, (2, 1, 3))]
    other_picked = cross(after(picked, own), 1)
    mine = after(mine, *came)
    theirs = cross(mine, 1)
    weight, act, slope = call(pre_body, [((4, WIDE, WIDE), bf16), wide, wide], *hiddens, mine, theirs, flops=3 * 10**8)
    saved = [saved[0]] + [cross(after(saved[x], own), x) for x in (1, 2, 3)]
    proj, sums = call(sums_body, [wide, ((8, TOK), f32)], own, *came, act)

    cgrad, qgrad, own, sgate, *parts = call(
        first_body,
        [wide, block, wide, block, block, block, block],
        after(sums, *saved, other_picked),
        *[shift(sums, "mp", d) for d in (2, 1, 3)],
        token_weight.reshape(1, TOK),
        act,
        proj,
        slope,
        weight,
        flops=3 * 10**8,
    )
    for step in range(section_count):
        if step > 0:
            own, sgate, *parts = call(
                step_body,
                [wide, block, block, block, block],
                incoming,
                cgrad,
                slope,
                weight,
                flops=3 * 10**8,
            )
        last = step + 1 == section_count
        if last:
            gates = [sgate, cross(sgate, 1), cross(sgate, 2)]
            gates.append(cross(gates[2], 1))
            layer_own, *layer_parts = call(
                layer_grad_body, [wide, block, block, block], *gates, *saved, flops=3 * 10**8
            )
            parts = [after(part, layer_own) for part in parts]
        came = [shift(part, "mp", d) for part, d in zip(parts, (2, 1, 3))]
        result = (own + sum(x.astype(f32) for x in came)).astype(bf16)
        if not last:
            incoming = to_previous(result)
        if step == 0:
            start = after(qgrad, came[0])
            qgrads = [qgrad] + [shift(start, "mp", -d) for d in (1, 2, 3)]
            keep, give = call(split_body, [((TOK, 1024), bf16)] * 2, after(qgrads[0], incoming), *qgrads[1:], scratch=held)
            products = call(
                proj_grad_body,
                [((8 * TOK, 2048), bf16)],
                keep,
                cross(give, 1),
                picked,
                other_picked,
                limit=24,
            )
            grad_proj = sum_z(products[0])

    grad_proj = after(grad_proj, layer_own).astype(f32)
    grad_layer = after(layer_own, grad_proj, result)
    grad_layer = grad_layer + sum(to_pair(part, d).astype(f32) for part, d in zip(layer_parts, (1, 2, 3)))
    return (result[None], grad_layer[None], grad_proj[None])


def solution(mesh):
    placed = (
        P("section", "dp", "mp"),
        P(),
        P("section", "dp", "mp"),
        P("section", "dp", "mp"),
        P("section", None, "mp"),
        P("dp"),
    )
    return jax.shard_map(
        on_device,
        mesh=mesh,
        in_specs=placed,
        out_specs=(P("section", "dp", "mp"), P("section", "dp", "mp"), P("section", "dp", "mp")),
        check_vma=False,
    )
```

time: 428 us -> 180 us (0.42)
  waiting for transfers between devices: 324 us -> 70.5 us
  starting transfers between devices: 8.84 us -> 60.7 us
  blocking collectives: 36 us -> 0 us
  matrix products: 29 us -> 9.78 us
  Pallas kernels: 0 us -> 9.92 us
  other arithmetic: 8.99 us -> 3.78 us
  local copies, waits for them, and re-layouts: 6.25 us -> 10.6 us
    reduce_scatter x6 -> x1, waiting for transfers between devices: 183 us -> 0.01 us  [sum_z(): lax.psum_scatter(array, 'dp', scatter_dimension=0, tiled=True, axis_index...]
    all_gather x2 -> x1, waiting for transfers between devices: 67.6 us -> 0.01 us  [gather_z(): return lax.all_gather(array, 'dp', axis=0, axis_index_groups=along_z())]
    unnamed x10 -> x2, waiting for transfers between devices: 61.5 us -> 0.7 us
    ppermute x3 -> x43, waiting for transfers between devices: 11.8 us -> 69.8 us  [the longest x28 44.5 us: shift(): return lax.ppermute(array, axis, [(i, (i + by) % n) for i in range(n)])]
    ppermute x3 -> x43, starting transfers between devices: 8.48 us -> 60.6 us  [the longest x28 37.5 us: shift(): return lax.ppermute(array, axis, [(i, (i + by) % n) for i in range(n)])]
    all_gather x2 -> x0, blocking collectives: 27.5 us -> none  [the longest x1 14.2 us: on_device(): qgrad_full = lax.all_gather(qgrad, 'mp', axis=1, tiled=True)]
    dot_general x9 -> x4, matrix products: 29 us -> 9.78 us  [on_device(): jnp.einsum('te,ke->tk', picked, part, preferred_element_type=f32)]
    pallas_call x0 -> x13, Pallas kernels: none -> 9.92 us  [call(): pl.pallas_call(body, out_shape=[jax.ShapeDtypeStruct(shape, dtype) for sh...]
  transfers between devices with their start and end apart: 12 -> 45, of which waited for: 12 -> 28; matrix products, arithmetic and copies ran while one was open for 6% -> 6% of each run, Pallas kernels for 0% -> 4%
where the time goes in v1:
time: 180 us
  waiting for transfers between devices  70.5 us (39%)
  starting transfers between devices  60.7 us (34%)
  between operations  14.3 us (8%)
  local copies, waits for them, and re-layouts  10.6 us (6%)
  Pallas kernels  9.92 us (6%)
  matrix products  9.78 us (5%)
  other arithmetic  3.78 us (2%)
    ppermute x28, waiting for transfers between devices, shift(): return lax.ppermute(array, axis, [(i, (i + by) % n) for i in range(n)])  44.5 us
    ppermute x28, starting transfers between devices, shift(): return lax.ppermute(array, axis, [(i, (i + by) % n) for i in range(n)])  37.5 us
    ppermute x3, waiting for transfers between devices, to_pair(): return lax.ppermute(array, 'dp', [(i, (i + 4 * by) % n) for i in range(n)])  11.2 us
    unnamed x44, local copies, waits for them, and re-layouts  10.6 us
    pallas_call x13, Pallas kernels, call(): pl.pallas_call(body, out_shape=[jax.ShapeDtypeStruct(shape, dtype) for sh...  9.92 us
    ppermute x3, starting transfers between devices, to_pair(): return lax.ppermute(array, 'dp', [(i, (i + 4 * by) % n) for i in range(n)])  9.89 us
    dot_general x4, matrix products, on_device(): jnp.einsum('te,ke->tk', picked, part, preferred_element_type=f32)  9.78 us
    ppermute x9, waiting for transfers between devices, cross(): return lax.ppermute(array, 'dp', [(i, i ^ bits) for i in range(n)])  9.13 us
  transfers between devices with their start and end apart: 45, of which 28 were waited for; matrix products, arithmetic and copies ran while one was open for 6% of the time, Pallas kernels for 4%

profile of v1, /device:TPU:6, one launch (start us, length us, event | category | flops | bytes accessed | tf_op | source)
XLA Modules:
  0.0 179.6 jit_solution(10940435828401275455)
XLA Ops:
  10.5 2.3 %collective-permute-start = (bf16[64,2048]{1,0:T(8,128)(2,1)S(1)}, bf16[64,2048]{1,0:T(8,128)(2,1)S(1)}, u32[]{:S(2)}, u32[]{:S(2)}) collective-permute-start(bf16[64,2048]{1,0:T(8,128)(2,1)S(1)} %get-tuple-element.58), channel_id=1, source_target_pairs={{0,64},{64,128},{128,192},{192,0},{1,65},{65,129},{129,193},{193,1... | collective-permute-start | bytes 786440 | tf_op jit(solution)/shard_map/ppermute | solution.py:17
  12.8 5.8 %collective-permute-done.from_left = bf16[64,2048]{1,0:T(8,128)(2,1)S(1)} collective-permute-done((bf16[64,2048]{1,0:T(8,128)(2,1)S(1)}, bf16[64,2048]{1,0:T(8,128)(2,1)S(1)}, u32[]{:S(2)}, u32[]{:S(2)}) %collective-permute-start) | collective-permute-done | bytes 262176 | tf_op jit(solution)/shard_map/ppermute | solution.py:17
  18.6 1.8 collective-permute-done.1.from_right
  21.8 2.0 %collective-permute-start.6 = (bf16[128,2048]{1,0:T(8,128)(2,1)S(1)}, bf16[128,2048]{1,0:T(8,128)(2,1)S(1)}, u32[]{:S(2)}, u32[]{:S(2)}) collective-permute-start(bf16[128,2048]{1,0:T(8,128)(2,1)S(1)} %get-tuple-element.63), channel_id=1, source_target_pairs={{0,192},{64,0},{128,64},{192,128},{1,193},{65,1},{129,65},{193,129... | collective-permute-start | bytes 1572872 | tf_op jit(solution)/shard_map/ppermute | solution.py:17
  23.8 2.7 %collective-permute-start.2 = (bf16[128,512]{1,0:T(8,128)(2,1)}, bf16[128,512]{1,0:T(8,128)(2,1)S(1)}, u32[]{:S(2)}, u32[]{:S(2)}) collective-permute-start(bf16[128,512]{1,0:T(8,128)(2,1)} %bitcast.30), channel_id=1, source_target_pairs={{0,3},{1,0},{2,1},{3,2},{4,7},{5,4},{6,5},{7,6},{8,11},{9,8},{10,9... | collective-permute-start | bytes 393224 | tf_op jit(solution)/shard_map/ppermute | solution.py:17
  28.0 2.6 %collective-permute-done.2.h1 = bf16[128,512]{1,0:T(8,128)(2,1)S(1)} collective-permute-done((bf16[128,512]{1,0:T(8,128)(2,1)}, bf16[128,512]{1,0:T(8,128)(2,1)S(1)}, u32[]{:S(2)}, u32[]{:S(2)}) %collective-permute-start.2) | collective-permute-done | bytes 131104 | tf_op jit(solution)/shard_map/ppermute | solution.py:17
  30.7 2.5 %collective-permute-done.3.h2 = bf16[128,512]{1,0:T(8,128)(2,1)S(1)} collective-permute-done((bf16[128,512]{1,0:T(8,128)(2,1)}, bf16[128,512]{1,0:T(8,128)(2,1)S(1)}, u32[]{:S(2)}, u32[]{:S(2)}) %collective-permute-start.3) | collective-permute-done | bytes 131104 | tf_op jit(solution)/shard_map/ppermute | solution.py:17
  36.0 2.4 %fusion.12 = bf16[128,512]{1,0:T(8,128)(2,1)S(1)} fusion(bf16[128,2048]{1,0:T(8,128)(2,1)S(1)} %shard_map.87.picked, bf16[4,512,2048]{2,1,0:T(8,128)(2,1)} %bitcast.36, s32[]{:T(128)S(6)} %select_n.35), kind=kOutput, calls=%fused_computation.12 | convolution fusion | flops 268500992 | bytes 2752516 | tf_op jit(solution)/shard_map/te,ke->tk/dot_general | solution.py:245
  38.5 3.9 %collective-permute-start.7 = (bf16[128,512]{1,0:T(8,128)(2,1)S(1)}, bf16[128,512]{1,0:T(8,128)(2,1)S(1)}, u32[]{:S(2)}, u32[]{:S(2)}) collective-permute-start(bf16[128,512]{1,0:T(8,128)(2,1)S(1)} %fusion.12), channel_id=1, source_target_pairs={{0,2},{1,3},{2,0},{3,1},{4,6},{5,7},{6,4},{7,5},{8,10},{9,11},{10,... | collective-permute-start | bytes 393224 | tf_op jit(solution)/shard_map/ppermute | solution.py:17
  42.4 2.4 %fusion.15 = bf16[128,512]{1,0:T(8,128)(2,1)S(1)} fusion(bf16[128,2048]{1,0:T(8,128)(2,1)S(1)} %shard_map.87.picked, bf16[4,512,2048]{2,1,0:T(8,128)(2,1)} %bitcast.37, s32[]{:T(128)S(6)} %select_n.37), kind=kOutput, calls=%fused_computation.13 | convolution fusion | flops 268500992 | bytes 2752516 | tf_op jit(solution)/shard_map/te,ke->tk/dot_general | solution.py:245
  45.6 2.4 %fusion.18 = bf16[128,512]{1,0:T(8,128)(2,1)S(1)} fusion(bf16[128,2048]{1,0:T(8,128)(2,1)S(1)} %shard_map.87.picked, bf16[4,512,2048]{2,1,0:T(8,128)(2,1)} %bitcast.38, s32[]{:T(128)S(6)} %select_n.39), kind=kOutput, calls=%fused_computation.14 | convolution fusion | flops 268500992 | bytes 2752516 | tf_op jit(solution)/shard_map/te,ke->tk/dot_general | solution.py:245
  48.0 2.6 %collective-permute-start.9 = (bf16[128,512]{1,0:T(8,128)(2,1)S(1)}, bf16[128,512]{1,0:T(8,128)(2,1)S(1)}, u32[]{:S(2)}, u32[]{:S(2)}) collective-permute-start(bf16[128,512]{1,0:T(8,128)(2,1)S(1)} %fusion.18), channel_id=1, source_target_pairs={{0,3},{1,0},{2,1},{3,2},{4,7},{5,4},{6,5},{7,6},{8,11},{9,8},{10,9... | collective-permute-start | bytes 393224 | tf_op jit(solution)/shard_map/ppermute | solution.py:17
  51.8 1.4 collective-permute-done.9.c3
  53.9 2.5 %fusion.6.own = f32[128,512]{1,0:T(8,128)S(1)} fusion(bf16[128,2048]{1,0:T(8,128)(2,1)S(1)} %shard_map.87.picked, bf16[4,512,2048]{2,1,0:T(8,128)(2,1)} %bitcast.39, s32[]{:T(128)S(6)} %select_n.33), kind=kOutput, calls=%fused_computation.6 | convolution fusion | flops 268435456 | bytes 2883588 | tf_op jit(solution)/shard_map/te,ke->tk/dot_general | solution.py:245
  57.8 1.9 %collective-permute-start.12 = (bf16[128,512]{1,0:T(8,128)(2,1)S(1)}, bf16[128,512]{1,0:T(8,128)(2,1)S(1)}, u32[]{:S(2)}, u32[]{:S(2)}) collective-permute-start(bf16[128,512]{1,0:T(8,128)(2,1)S(1)} %get-tuple-element.71), channel_id=1, source_target_pairs={{0,8},{4,12},{8,0},{12,4},{16,24},{20,28},{24,16},{28,20},{32,40},... | collective-permute-start | bytes 393224 | tf_op jit(solution)/shard_map/ppermute | solution.py:39
  64.2 1.9 %collective-permute-start.15 = (f32[8,128]{1,0:T(8,128)S(1)}, f32[8,128]{1,0:T(8,128)S(1)}, u32[]{:S(2)}, u32[]{:S(2)}) collective-permute-start(f32[8,128]{1,0:T(8,128)S(1)} %get-tuple-element.75.s0), channel_id=1, source_target_pairs={{0,2},{1,3},{2,0},{3,1},{4,6},{5,7},{6,4},{7,5},{8,10},{9,11},{10,... | collective-permute-start | bytes 12296 | tf_op jit(solution)/shard_map/ppermute | solution.py:17
  66.2 2.6 %collective-permute-start.16 = (f32[8,128]{1,0:T(8,128)S(1)}, f32[8,128]{1,0:T(8,128)S(1)}, u32[]{:S(2)}, u32[]{:S(2)}) collective-permute-start(f32[8,128]{1,0:T(8,128)S(1)} %get-tuple-element.75.s0), channel_id=1, source_target_pairs={{0,1},{1,2},{2,3},{3,0},{4,5},{5,6},{6,7},{7,4},{8,9},{9,10},{10,1... | collective-permute-start | bytes 12296 | tf_op jit(solution)/shard_map/ppermute | solution.py:17
  69.5 1.6 collective-permute-done.16.s2
  71.0 1.4 collective-permute-done.17.s3
  72.4 1.5 shard_map.91
  74.0 1.8 %collective-permute-start.20 = (bf16[128,512]{1,0:T(8,128)(2,1)S(1)}, bf16[128,512]{1,0:T(8,128)(2,1)S(1)}, u32[]{:S(2)}, u32[]{:S(2)}) collective-permute-start(bf16[128,512]{1,0:T(8,128)(2,1)S(1)} %get-tuple-element.82), channel_id=1, source_target_pairs={{0,3},{1,0},{2,1},{3,2},{4,7},{5,4},{6,5},{7,6},{8,11},{9,8},{10,9... | collective-permute-start | bytes 393224 | tf_op jit(solution)/shard_map/ppermute | solution.py:17
  77.2 2.5 %collective-permute-done.20 = bf16[128,512]{1,0:T(8,128)(2,1)S(1)} collective-permute-done((bf16[128,512]{1,0:T(8,128)(2,1)S(1)}, bf16[128,512]{1,0:T(8,128)(2,1)S(1)}, u32[]{:S(2)}, u32[]{:S(2)}) %collective-permute-start.20) | collective-permute-done | bytes 131104 | tf_op jit(solution)/shard_map/ppermute | solution.py:17
  79.7 4.0 %collective-permute-done.19 = bf16[128,512]{1,0:T(8,128)(2,1)S(1)} collective-permute-done((bf16[128,512]{1,0:T(8,128)(2,1)S(1)}, bf16[128,512]{1,0:T(8,128)(2,1)S(1)}, u32[]{:S(2)}, u32[]{:S(2)}) %collective-permute-start.19) | collective-permute-done | bytes 131104 | tf_op jit(solution)/shard_map/ppermute | solution.py:17
  83.7 2.1 %collective-permute-start.21 = (bf16[128,512]{1,0:T(8,128)(2,1)S(1)}, bf16[128,512]{1,0:T(8,128)(2,1)S(1)}, u32[]{:S(2)}, u32[]{:S(2)}) collective-permute-start(bf16[128,512]{1,0:T(8,128)(2,1)S(1)} %add_convert_fusion.3), channel_id=1, source_target_pairs={{64,0},{128,64},{192,128},{65,1},{129,65},{193,129},{66,2},{130,66... | collective-permute-start | bytes 393224 | tf_op jit(solution)/shard_map/ppermute | solution.py:22
  85.9 1.9 %collective-permute-start.36 = (bf16[128,512]{1,0:T(8,128)(2,1)S(1)}, bf16[128,512]{1,0:T(8,128)(2,1)S(1)}, u32[]{:S(2)}, u32[]{:S(2)}) collective-permute-start(bf16[128,512]{1,0:T(8,128)(2,1)S(1)} %get-tuple-element.103.q0), channel_id=1, source_target_pairs={{0,3},{1,0},{2,1},{3,2},{4,7},{5,4},{6,5},{7,6},{8,11},{9,8},{10,9... | collective-permute-start | bytes 393224 | tf_op jit(solution)/shard_map/ppermute | solution.py:17
  88.7 3.0 %collective-permute-done.36.q1 = bf16[128,512]{1,0:T(8,128)(2,1)S(1)} collective-permute-done((bf16[128,512]{1,0:T(8,128)(2,1)S(1)}, bf16[128,512]{1,0:T(8,128)(2,1)S(1)}, u32[]{:S(2)}, u32[]{:S(2)}) %collective-permute-start.36) | collective-permute-done | bytes 131104 | tf_op jit(solution)/shard_map/ppermute | solution.py:17
  91.7 2.7 %collective-permute-done.37.q2 = bf16[128,512]{1,0:T(8,128)(2,1)S(1)} collective-permute-done((bf16[128,512]{1,0:T(8,128)(2,1)S(1)}, bf16[128,512]{1,0:T(8,128)(2,1)S(1)}, u32[]{:S(2)}, u32[]{:S(2)}) %collective-permute-start.37) | collective-permute-done | bytes 131104 | tf_op jit(solution)/shard_map/ppermute | solution.py:17
  95.6 1.5 collective-permute-done.39.came
  98.5 2.0 %copy-done = bf16[1024,2048]{1,0:T(8,128)(2,1)} copy-done((bf16[1024,2048]{1,0:T(8,128)(2,1)}, bf16[1024,2048]{1,0:T(8,128)(2,1)S(1)}, u32[]{:S(2)}) %copy-start) | copy-done | bytes 4194328
  104.8 2.9 %collective-permute-done.24 = bf16[128,512]{1,0:T(8,128)(2,1)S(1)} collective-permute-done((bf16[128,512]{1,0:T(8,128)(2,1)S(1)}, bf16[128,512]{1,0:T(8,128)(2,1)S(1)}, u32[]{:S(2)}, u32[]{:S(2)}) %collective-permute-start.24) | collective-permute-done | bytes 131104 | tf_op jit(solution)/shard_map/ppermute | solution.py:17
  107.8 4.3 %collective-permute-done.23 = bf16[128,512]{1,0:T(8,128)(2,1)S(1)} collective-permute-done((bf16[128,512]{1,0:T(8,128)(2,1)S(1)}, bf16[128,512]{1,0:T(8,128)(2,1)S(1)}, u32[]{:S(2)}, u32[]{:S(2)}) %collective-permute-start.23) | collective-permute-done | bytes 131104 | tf_op jit(solution)/shard_map/ppermute | solution.py:17
  112.1 2.2 %collective-permute-start.25 = (bf16[128,512]{1,0:T(8,128)(2,1)S(1)}, bf16[128,512]{1,0:T(8,128)(2,1)S(1)}, u32[]{:S(2)}, u32[]{:S(2)}) collective-permute-start(bf16[128,512]{1,0:T(8,128)(2,1)S(1)} %add_convert_fusion.2), channel_id=1, source_target_pairs={{64,0},{128,64},{192,128},{65,1},{129,65},{193,129},{66,2},{130,66... | collective-permute-start | bytes 393224 | tf_op jit(solution)/shard_map/ppermute | solution.py:22
  114.4 2.5 %collective-permute-done.25.incoming = bf16[128,512]{1,0:T(8,128)(2,1)S(1)} collective-permute-done((bf16[128,512]{1,0:T(8,128)(2,1)S(1)}, bf16[128,512]{1,0:T(8,128)(2,1)S(1)}, u32[]{:S(2)}, u32[]{:S(2)}) %collective-permute-start.25) | collective-permute-done | bytes 131104 | tf_op jit(solution)/shard_map/ppermute | solution.py:22
  120.2 1.4 collective-permute-start.26
  121.6 2.5 %collective-permute-done.28 = bf16[128,512]{1,0:T(8,128)(2,1)S(1)} collective-permute-done((bf16[128,512]{1,0:T(8,128)(2,1)S(1)}, bf16[128,512]{1,0:T(8,128)(2,1)S(1)}, u32[]{:S(2)}, u32[]{:S(2)}) %collective-permute-start.28) | collective-permute-done | bytes 131104 | tf_op jit(solution)/shard_map/ppermute | solution.py:17
  125.2 1.5 collective-permute-done.26
  126.7 4.4 %collective-permute-start.29 = (bf16[128,512]{1,0:T(8,128)(2,1)S(1)}, bf16[128,512]{1,0:T(8,128)(2,1)S(1)}, u32[]{:S(2)}, u32[]{:S(2)}) collective-permute-start(bf16[128,512]{1,0:T(8,128)(2,1)S(1)} %add_convert_fusion.1), channel_id=1, source_target_pairs={{64,0},{128,64},{192,128},{65,1},{129,65},{193,129},{66,2},{130,66... | collective-permute-start | bytes 393224 | tf_op jit(solution)/shard_map/ppermute | solution.py:22
  131.1 2.5 %collective-permute-done.29.incoming = bf16[128,512]{1,0:T(8,128)(2,1)S(1)} collective-permute-done((bf16[128,512]{1,0:T(8,128)(2,1)S(1)}, bf16[128,512]{1,0:T(8,128)(2,1)S(1)}, u32[]{:S(2)}, u32[]{:S(2)}) %collective-permute-start.29) | collective-permute-done | bytes 131104 | tf_op jit(solution)/shard_map/ppermute | solution.py:22
  134.4 1.8 collective-permute-start.31
  136.2 6.2 %collective-permute-done.31.g2 = bf16[128,512]{1,0:T(8,128)(2,1)S(1)} collective-permute-done((bf16[128,512]{1,0:T(8,128)(2,1)S(1)}, bf16[128,512]{1,0:T(8,128)(2,1)S(1)}, u32[]{:S(2)}, u32[]{:S(2)}) %collective-permute-start.31) | collective-permute-done | bytes 131104 | tf_op jit(solution)/shard_map/ppermute | solution.py:39
  142.5 1.3 collective-permute-done.32.g3
  144.3 2.2 %collective-permute-start.35 = (bf16[128,512]{1,0:T(8,128)(2,1)S(1)}, bf16[128,512]{1,0:T(8,128)(2,1)S(1)}, u32[]{:S(2)}, u32[]{:S(2)}) collective-permute-start(bf16[128,512]{1,0:T(8,128)(2,1)S(1)} %get-tuple-element.100), channel_id=1, source_target_pairs={{0,3},{1,0},{2,1},{3,2},{4,7},{5,4},{6,5},{7,6},{8,11},{9,8},{10,9... | collective-permute-start | bytes 393224 | tf_op jit(solution)/shard_map/ppermute | solution.py:17
  146.5 1.6 collective-permute-start.33
  148.0 6.1 %collective-permute-start.42 = (bf16[128,512]{1,0:T(8,128)(2,1)S(1)}, bf16[128,512]{1,0:T(8,128)(2,1)S(1)}, u32[]{:S(2)}, u32[]{:S(2)}) collective-permute-start(bf16[128,512]{1,0:T(8,128)(2,1)S(1)} %get-tuple-element.110), channel_id=1, source_target_pairs={{0,48},{4,52},{8,56},{12,60},{16,0},{20,4},{24,8},{28,12},{32,16},... | collective-permute-start | bytes 393224 | tf_op jit(solution)/shard_map/ppermute | solution.py:44
  155.0 2.9 %collective-permute-start.40 = (bf16[128,512]{1,0:T(8,128)(2,1)S(1)}, bf16[128,512]{1,0:T(8,128)(2,1)S(1)}, u32[]{:S(2)}, u32[]{:S(2)}) collective-permute-start(bf16[128,512]{1,0:T(8,128)(2,1)S(1)} %get-tuple-element.108), channel_id=1, source_target_pairs={{0,16},{4,20},{8,24},{12,28},{16,32},{20,36},{24,40},{28,44},{32,4... | collective-permute-start | bytes 393224 | tf_op jit(solution)/shard_map/ppermute | solution.py:44
  158.6 1.6 collective-permute-done.42
  160.2 8.6 %collective-permute-done.41 = bf16[128,512]{1,0:T(8,128)(2,1)S(1)} collective-permute-done((bf16[128,512]{1,0:T(8,128)(2,1)S(1)}, bf16[128,512]{1,0:T(8,128)(2,1)S(1)}, u32[]{:S(2)}, u32[]{:S(2)}) %collective-permute-start.41) | collective-permute-done | bytes 131104 | tf_op jit(solution)/shard_map/ppermute | solution.py:44
  170.6 2.1 %convert_bitcast_fusion = f32[1,128,2048]{2,1,0:T(8,128)} fusion(bf16[128,2048]{1,0:T(8,128)(2,1)} %reduce-scatter.2.cloned.1.call-done), kind=kLoop, calls=%fused_computation.16 | loop fusion | flops 262144 | bytes 1572864 | tf_op jit(solution)/shard_map/broadcast_in_dim | solution.py:308
  (111 shorter events, 36.7 us)
Async XLA Ops:
  7.2 46.7 %all-gather.2.cloned.1.call-start = ((), (), s32[]{:S(2)}) async-start(), calls=%async_computation.1 | async-start | bytes 1179648 | tf_op jit(solution)/shard_map/all_gather | solution.py:30
  7.9 162.7 %reduce-scatter.2.cloned.1.call-start = ((), (), s32[]{:S(2)}) async-start(), calls=%async_computation.2 | async-start | bytes 4718592 | tf_op jit(solution)/shard_map/reduce_scatter | solution.py:34
  10.5 8.1 %collective-permute-start = (bf16[64,2048]{1,0:T(8,128)(2,1)S(1)}, bf16[64,2048]{1,0:T(8,128)(2,1)S(1)}, u32[]{:S(2)}, u32[]{:S(2)}) collective-permute-start(bf16[64,2048]{1,0:T(8,128)(2,1)S(1)} %get-tuple-element.58), channel_id=1, source_target_pairs={{0,64},{64,128},{128,192},{192,0},{1,65},{65,129},{129,193},{193,1... | collective-permute-start | bytes 786440 | tf_op jit(solution)/shard_map/ppermute | solution.py:17
  12.7 7.6 %collective-permute-start.1 = (bf16[64,2048]{1,0:T(8,128)(2,1)S(1)}, bf16[64,2048]{1,0:T(8,128)(2,1)S(1)}, u32[]{:S(2)}, u32[]{:S(2)}) collective-permute-start(bf16[64,2048]{1,0:T(8,128)(2,1)S(1)} %get-tuple-element.59), channel_id=1, source_target_pairs={{0,192},{64,0},{128,64},{192,128},{1,193},{65,1},{129,65},{193,129... | collective-permute-start | bytes 786440 | tf_op jit(solution)/shard_map/ppermute | solution.py:17
  21.7 12.9 %collective-permute-start.5 = (bf16[128,2048]{1,0:T(8,128)(2,1)S(1)}, bf16[128,2048]{1,0:T(8,128)(2,1)S(1)}, u32[]{:S(2)}, u32[]{:S(2)}) collective-permute-start(bf16[128,2048]{1,0:T(8,128)(2,1)S(1)} %get-tuple-element.60), channel_id=1, source_target_pairs={{0,64},{64,128},{128,192},{192,0},{1,65},{65,129},{129,193},{193,1... | collective-permute-start | bytes 1572872 | tf_op jit(solution)/shard_map/ppermute | solution.py:17
  21.8 13.0 %collective-permute-start.6 = (bf16[128,2048]{1,0:T(8,128)(2,1)S(1)}, bf16[128,2048]{1,0:T(8,128)(2,1)S(1)}, u32[]{:S(2)}, u32[]{:S(2)}) collective-permute-start(bf16[128,2048]{1,0:T(8,128)(2,1)S(1)} %get-tuple-element.63), channel_id=1, source_target_pairs={{0,192},{64,0},{128,64},{192,128},{1,193},{65,1},{129,65},{193,129... | collective-permute-start | bytes 1572872 | tf_op jit(solution)/shard_map/ppermute | solution.py:17
  23.8 6.9 %collective-permute-start.2 = (bf16[128,512]{1,0:T(8,128)(2,1)}, bf16[128,512]{1,0:T(8,128)(2,1)S(1)}, u32[]{:S(2)}, u32[]{:S(2)}) collective-permute-start(bf16[128,512]{1,0:T(8,128)(2,1)} %bitcast.30), channel_id=1, source_target_pairs={{0,3},{1,0},{2,1},{3,2},{4,7},{5,4},{6,5},{7,6},{8,11},{9,8},{10,9... | collective-permute-start | bytes 393224 | tf_op jit(solution)/shard_map/ppermute | solution.py:17
  26.4 6.8 %collective-permute-start.3 = (bf16[128,512]{1,0:T(8,128)(2,1)}, bf16[128,512]{1,0:T(8,128)(2,1)S(1)}, u32[]{:S(2)}, u32[]{:S(2)}) collective-permute-start(bf16[128,512]{1,0:T(8,128)(2,1)} %bitcast.31), channel_id=1, source_target_pairs={{0,2},{1,3},{2,0},{3,1},{4,6},{5,7},{6,4},{7,5},{8,10},{9,11},{10,... | collective-permute-start | bytes 393224 | tf_op jit(solution)/shard_map/ppermute | solution.py:17
  27.1 7.5 %collective-permute-start.4 = (bf16[128,512]{1,0:T(8,128)(2,1)}, bf16[128,512]{1,0:T(8,128)(2,1)S(1)}, u32[]{:S(2)}, u32[]{:S(2)}) collective-permute-start(bf16[128,512]{1,0:T(8,128)(2,1)} %bitcast.32), channel_id=1, source_target_pairs={{0,1},{1,2},{2,3},{3,0},{4,5},{5,6},{6,7},{7,4},{8,9},{9,10},{10,1... | collective-permute-start | bytes 393224 | tf_op jit(solution)/shard_map/ppermute | solution.py:17
  38.5 12.2 %collective-permute-start.7 = (bf16[128,512]{1,0:T(8,128)(2,1)S(1)}, bf16[128,512]{1,0:T(8,128)(2,1)S(1)}, u32[]{:S(2)}, u32[]{:S(2)}) collective-permute-start(bf16[128,512]{1,0:T(8,128)(2,1)S(1)} %fusion.12), channel_id=1, source_target_pairs={{0,2},{1,3},{2,0},{3,1},{4,6},{5,7},{6,4},{7,5},{8,10},{9,11},{10,... | collective-permute-start | bytes 393224 | tf_op jit(solution)/shard_map/ppermute | solution.py:17
  44.9 6.3 %collective-permute-start.8 = (bf16[128,512]{1,0:T(8,128)(2,1)S(1)}, bf16[128,512]{1,0:T(8,128)(2,1)S(1)}, u32[]{:S(2)}, u32[]{:S(2)}) collective-permute-start(bf16[128,512]{1,0:T(8,128)(2,1)S(1)} %fusion.15), channel_id=1, source_target_pairs={{0,1},{1,2},{2,3},{3,0},{4,5},{5,6},{6,7},{7,4},{8,9},{9,10},{10,1... | collective-permute-start | bytes 393224 | tf_op jit(solution)/shard_map/ppermute | solution.py:17
  48.0 5.2 %collective-permute-start.9 = (bf16[128,512]{1,0:T(8,128)(2,1)S(1)}, bf16[128,512]{1,0:T(8,128)(2,1)S(1)}, u32[]{:S(2)}, u32[]{:S(2)}) collective-permute-start(bf16[128,512]{1,0:T(8,128)(2,1)S(1)} %fusion.18), channel_id=1, source_target_pairs={{0,3},{1,0},{2,1},{3,2},{4,7},{5,4},{6,5},{7,6},{8,11},{9,8},{10,9... | collective-permute-start | bytes 393224 | tf_op jit(solution)/shard_map/ppermute | solution.py:17
  53.9 5.9 %collective-permute-start.10 = (bf16[8,128,512]{2,1,0:T(8,128)(2,1)}, bf16[8,128,512]{2,1,0:T(8,128)(2,1)S(1)}, u32[]{:S(2)}, u32[]{:S(2)}) collective-permute-start(bf16[8,128,512]{2,1,0:T(8,128)(2,1)} %all-gather.2.cloned.1.call-done.mine), channel_id=1, source_target_pairs={{0,4},{4,0},{8,12},{12,8},{16,20},{20,16},{24,28},{28,24},{32,36},... | collective-permute-start | bytes 3145736 | tf_op jit(solution)/shard_map/ppermute | solution.py:39
  56.4 13.1 %collective-permute-start.14 = (bf16[128,2048]{1,0:T(8,128)(2,1)S(1)}, bf16[128,2048]{1,0:T(8,128)(2,1)S(1)}, u32[]{:S(2)}, u32[]{:S(2)}) collective-permute-start(bf16[128,2048]{1,0:T(8,128)(2,1)S(1)} %shard_map.87.picked), channel_id=1, source_target_pairs={{0,4},{4,0},{8,12},{12,8},{16,20},{20,16},{24,28},{28,24},{32,36},... | collective-permute-start | bytes 1572872 | tf_op jit(solution)/shard_map/ppermute | solution.py:39
  57.7 8.5 %collective-permute-start.11 = (bf16[128,512]{1,0:T(8,128)(2,1)S(1)}, bf16[128,512]{1,0:T(8,128)(2,1)S(1)}, u32[]{:S(2)}, u32[]{:S(2)}) collective-permute-start(bf16[128,512]{1,0:T(8,128)(2,1)S(1)} %get-tuple-element.69), channel_id=1, source_target_pairs={{0,4},{4,0},{8,12},{12,8},{16,20},{20,16},{24,28},{28,24},{32,36},... | collective-permute-start | bytes 393224 | tf_op jit(solution)/shard_map/ppermute | solution.py:39
  57.8 11.1 %collective-permute-start.12 = (bf16[128,512]{1,0:T(8,128)(2,1)S(1)}, bf16[128,512]{1,0:T(8,128)(2,1)S(1)}, u32[]{:S(2)}, u32[]{:S(2)}) collective-permute-start(bf16[128,512]{1,0:T(8,128)(2,1)S(1)} %get-tuple-element.71), channel_id=1, source_target_pairs={{0,8},{4,12},{8,0},{12,4},{16,24},{20,28},{24,16},{28,20},{32,40},... | collective-permute-start | bytes 393224 | tf_op jit(solution)/shard_map/ppermute | solution.py:39
  59.7 9.7 %collective-permute-start.13 = (bf16[128,512]{1,0:T(8,128)(2,1)S(1)}, bf16[128,512]{1,0:T(8,128)(2,1)S(1)}, u32[]{:S(2)}, u32[]{:S(2)}) collective-permute-start(bf16[128,512]{1,0:T(8,128)(2,1)S(1)} %get-tuple-element.73), channel_id=1, source_target_pairs={{0,12},{4,8},{8,4},{12,0},{16,28},{20,24},{24,20},{28,16},{32,44},... | collective-permute-start | bytes 393224 | tf_op jit(solution)/shard_map/ppermute | solution.py:39
  64.2 5.2 %collective-permute-start.15 = (f32[8,128]{1,0:T(8,128)S(1)}, f32[8,128]{1,0:T(8,128)S(1)}, u32[]{:S(2)}, u32[]{:S(2)}) collective-permute-start(f32[8,128]{1,0:T(8,128)S(1)} %get-tuple-element.75.s0), channel_id=1, source_target_pairs={{0,2},{1,3},{2,0},{3,1},{4,6},{5,7},{6,4},{7,5},{8,10},{9,11},{10,... | collective-permute-start | bytes 12296 | tf_op jit(solution)/shard_map/ppermute | solution.py:17
  66.2 4.8 %collective-permute-start.16 = (f32[8,128]{1,0:T(8,128)S(1)}, f32[8,128]{1,0:T(8,128)S(1)}, u32[]{:S(2)}, u32[]{:S(2)}) collective-permute-start(f32[8,128]{1,0:T(8,128)S(1)} %get-tuple-element.75.s0), channel_id=1, source_target_pairs={{0,1},{1,2},{2,3},{3,0},{4,5},{5,6},{6,7},{7,4},{8,9},{9,10},{10,1... | collective-permute-start | bytes 12296 | tf_op jit(solution)/shard_map/ppermute | solution.py:17
  68.8 3.6 %collective-permute-start.17 = (f32[8,128]{1,0:T(8,128)S(1)}, f32[8,128]{1,0:T(8,128)S(1)}, u32[]{:S(2)}, u32[]{:S(2)}) collective-permute-start(f32[8,128]{1,0:T(8,128)S(1)} %get-tuple-element.75.s0), channel_id=1, source_target_pairs={{0,3},{1,0},{2,1},{3,2},{4,7},{5,4},{6,5},{7,6},{8,11},{9,8},{10,9... | collective-permute-start | bytes 12296 | tf_op jit(solution)/shard_map/ppermute | solution.py:17
  74.0 5.7 %collective-permute-start.20 = (bf16[128,512]{1,0:T(8,128)(2,1)S(1)}, bf16[128,512]{1,0:T(8,128)(2,1)S(1)}, u32[]{:S(2)}, u32[]{:S(2)}) collective-permute-start(bf16[128,512]{1,0:T(8,128)(2,1)S(1)} %get-tuple-element.82), channel_id=1, source_target_pairs={{0,3},{1,0},{2,1},{3,2},{4,7},{5,4},{6,5},{7,6},{8,11},{9,8},{10,9... | collective-permute-start | bytes 393224 | tf_op jit(solution)/shard_map/ppermute | solution.py:17
  75.8 7.9 %collective-permute-start.19 = (bf16[128,512]{1,0:T(8,128)(2,1)S(1)}, bf16[128,512]{1,0:T(8,128)(2,1)S(1)}, u32[]{:S(2)}, u32[]{:S(2)}) collective-permute-start(bf16[128,512]{1,0:T(8,128)(2,1)S(1)} %get-tuple-element.81), channel_id=1, source_target_pairs={{0,1},{1,2},{2,3},{3,0},{4,5},{5,6},{6,7},{7,4},{8,9},{9,10},{10,1... | collective-permute-start | bytes 393224 | tf_op jit(solution)/shard_map/ppermute | solution.py:17
  76.0 7.7 %collective-permute-start.18 = (bf16[128,512]{1,0:T(8,128)(2,1)S(1)}, bf16[128,512]{1,0:T(8,128)(2,1)S(1)}, u32[]{:S(2)}, u32[]{:S(2)}) collective-permute-start(bf16[128,512]{1,0:T(8,128)(2,1)S(1)} %get-tuple-element.80), channel_id=1, source_target_pairs={{0,2},{1,3},{2,0},{3,1},{4,6},{5,7},{6,4},{7,5},{8,10},{9,11},{10,... | collective-permute-start | bytes 393224 | tf_op jit(solution)/shard_map/ppermute | solution.py:17
  83.7 5.0 %collective-permute-start.21 = (bf16[128,512]{1,0:T(8,128)(2,1)S(1)}, bf16[128,512]{1,0:T(8,128)(2,1)S(1)}, u32[]{:S(2)}, u32[]{:S(2)}) collective-permute-start(bf16[128,512]{1,0:T(8,128)(2,1)S(1)} %add_convert_fusion.3), channel_id=1, source_target_pairs={{64,0},{128,64},{192,128},{65,1},{129,65},{193,129},{66,2},{130,66... | collective-permute-start | bytes 393224 | tf_op jit(solution)/shard_map/ppermute | solution.py:22
  85.9 5.8 %collective-permute-start.36 = (bf16[128,512]{1,0:T(8,128)(2,1)S(1)}, bf16[128,512]{1,0:T(8,128)(2,1)S(1)}, u32[]{:S(2)}, u32[]{:S(2)}) collective-permute-start(bf16[128,512]{1,0:T(8,128)(2,1)S(1)} %get-tuple-element.103.q0), channel_id=1, source_target_pairs={{0,3},{1,0},{2,1},{3,2},{4,7},{5,4},{6,5},{7,6},{8,11},{9,8},{10,9... | collective-permute-start | bytes 393224 | tf_op jit(solution)/shard_map/ppermute | solution.py:17
  87.8 6.6 %collective-permute-start.37 = (bf16[128,512]{1,0:T(8,128)(2,1)S(1)}, bf16[128,512]{1,0:T(8,128)(2,1)S(1)}, u32[]{:S(2)}, u32[]{:S(2)}) collective-permute-start(bf16[128,512]{1,0:T(8,128)(2,1)S(1)} %get-tuple-element.103.q0), channel_id=1, source_target_pairs={{0,2},{1,3},{2,0},{3,1},{4,6},{5,7},{6,4},{7,5},{8,10},{9,11},{10,... | collective-permute-start | bytes 393224 | tf_op jit(solution)/shard_map/ppermute | solution.py:17
  87.8 7.6 %collective-permute-start.38 = (bf16[128,512]{1,0:T(8,128)(2,1)S(1)}, bf16[128,512]{1,0:T(8,128)(2,1)S(1)}, u32[]{:S(2)}, u32[]{:S(2)}) collective-permute-start(bf16[128,512]{1,0:T(8,128)(2,1)S(1)} %get-tuple-element.103.q0), channel_id=1, source_target_pairs={{0,1},{1,2},{2,3},{3,0},{4,5},{5,6},{6,7},{7,4},{8,9},{9,10},{10,1... | collective-permute-start | bytes 393224 | tf_op jit(solution)/shard_map/ppermute | solution.py:17
  95.5 1.6 collective-permute-start.39
  101.8 42.0 %copy-start.17 = (bf16[128,512]{1,0:T(8,128)(2,1)S(1)}, bf16[128,512]{1,0:T(8,128)(2,1)}, u32[]{:S(2)}) copy-start(bf16[128,512]{1,0:T(8,128)(2,1)} %copy-done.16) | copy-start | bytes 393220
  101.8 42.0 %copy-start.19 = (bf16[128,512]{1,0:T(8,128)(2,1)S(1)}, bf16[128,512]{1,0:T(8,128)(2,1)}, u32[]{:S(2)}) copy-start(bf16[128,512]{1,0:T(8,128)(2,1)} %copy-done.18) | copy-start | bytes 393220
  101.8 42.0 %copy-start.21 = (bf16[128,512]{1,0:T(8,128)(2,1)S(1)}, bf16[128,512]{1,0:T(8,128)(2,1)}, u32[]{:S(2)}) copy-start(bf16[128,512]{1,0:T(8,128)(2,1)} %copy-done.20) | copy-start | bytes 393220
  101.8 5.9 %collective-permute-start.24 = (bf16[128,512]{1,0:T(8,128)(2,1)S(1)}, bf16[128,512]{1,0:T(8,128)(2,1)S(1)}, u32[]{:S(2)}, u32[]{:S(2)}) collective-permute-start(bf16[128,512]{1,0:T(8,128)(2,1)S(1)} %get-tuple-element.87), channel_id=1, source_target_pairs={{0,3},{1,0},{2,1},{3,2},{4,7},{5,4},{6,5},{7,6},{8,11},{9,8},{10,9... | collective-permute-start | bytes 393224 | tf_op jit(solution)/shard_map/ppermute | solution.py:17
  102.8 9.3 %collective-permute-start.23 = (bf16[128,512]{1,0:T(8,128)(2,1)S(1)}, bf16[128,512]{1,0:T(8,128)(2,1)S(1)}, u32[]{:S(2)}, u32[]{:S(2)}) collective-permute-start(bf16[128,512]{1,0:T(8,128)(2,1)S(1)} %get-tuple-element.86), channel_id=1, source_target_pairs={{0,1},{1,2},{2,3},{3,0},{4,5},{5,6},{6,7},{7,4},{8,9},{9,10},{10,1... | collective-permute-start | bytes 393224 | tf_op jit(solution)/shard_map/ppermute | solution.py:17
  103.9 8.1 %collective-permute-start.22 = (bf16[128,512]{1,0:T(8,128)(2,1)S(1)}, bf16[128,512]{1,0:T(8,128)(2,1)S(1)}, u32[]{:S(2)}, u32[]{:S(2)}) collective-permute-start(bf16[128,512]{1,0:T(8,128)(2,1)S(1)} %get-tuple-element.85), channel_id=1, source_target_pairs={{0,2},{1,3},{2,0},{3,1},{4,6},{5,7},{6,4},{7,5},{8,10},{9,11},{10,... | collective-permute-start | bytes 393224 | tf_op jit(solution)/shard_map/ppermute | solution.py:17
  112.1 4.7 %collective-permute-start.25 = (bf16[128,512]{1,0:T(8,128)(2,1)S(1)}, bf16[128,512]{1,0:T(8,128)(2,1)S(1)}, u32[]{:S(2)}, u32[]{:S(2)}) collective-permute-start(bf16[128,512]{1,0:T(8,128)(2,1)S(1)} %add_convert_fusion.2), channel_id=1, source_target_pairs={{64,0},{128,64},{192,128},{65,1},{129,65},{193,129},{66,2},{130,66... | collective-permute-start | bytes 393224 | tf_op jit(solution)/shard_map/ppermute | solution.py:22
  118.2 6.0 %collective-permute-start.28 = (bf16[128,512]{1,0:T(8,128)(2,1)S(1)}, bf16[128,512]{1,0:T(8,128)(2,1)S(1)}, u32[]{:S(2)}, u32[]{:S(2)}) collective-permute-start(bf16[128,512]{1,0:T(8,128)(2,1)S(1)} %get-tuple-element.91), channel_id=1, source_target_pairs={{0,3},{1,0},{2,1},{3,2},{4,7},{5,4},{6,5},{7,6},{8,11},{9,8},{10,9... | collective-permute-start | bytes 393224 | tf_op jit(solution)/shard_map/ppermute | solution.py:17
  119.0 6.2 %collective-permute-start.27 = (bf16[128,512]{1,0:T(8,128)(2,1)S(1)}, bf16[128,512]{1,0:T(8,128)(2,1)S(1)}, u32[]{:S(2)}, u32[]{:S(2)}) collective-permute-start(bf16[128,512]{1,0:T(8,128)(2,1)S(1)} %get-tuple-element.90), channel_id=1, source_target_pairs={{0,1},{1,2},{2,3},{3,0},{4,5},{5,6},{6,7},{7,4},{8,9},{9,10},{10,1... | collective-permute-start | bytes 393224 | tf_op jit(solution)/shard_map/ppermute | solution.py:17
  120.2 6.5 %collective-permute-start.26 = (bf16[128,512]{1,0:T(8,128)(2,1)S(1)}, bf16[128,512]{1,0:T(8,128)(2,1)S(1)}, u32[]{:S(2)}, u32[]{:S(2)}) collective-permute-start(bf16[128,512]{1,0:T(8,128)(2,1)S(1)} %get-tuple-element.89), channel_id=1, source_target_pairs={{0,2},{1,3},{2,0},{3,1},{4,6},{5,7},{6,4},{7,5},{8,10},{9,11},{10,... | collective-permute-start | bytes 393224 | tf_op jit(solution)/shard_map/ppermute | solution.py:17
  126.7 6.9 %collective-permute-start.29 = (bf16[128,512]{1,0:T(8,128)(2,1)S(1)}, bf16[128,512]{1,0:T(8,128)(2,1)S(1)}, u32[]{:S(2)}, u32[]{:S(2)}) collective-permute-start(bf16[128,512]{1,0:T(8,128)(2,1)S(1)} %add_convert_fusion.1), channel_id=1, source_target_pairs={{64,0},{128,64},{192,128},{65,1},{129,65},{193,129},{66,2},{130,66... | collective-permute-start | bytes 393224 | tf_op jit(solution)/shard_map/ppermute | solution.py:22
  134.4 8.0 %collective-permute-start.31 = (bf16[128,512]{1,0:T(8,128)(2,1)S(1)}, bf16[128,512]{1,0:T(8,128)(2,1)S(1)}, u32[]{:S(2)}, u32[]{:S(2)}) collective-permute-start(bf16[128,512]{1,0:T(8,128)(2,1)S(1)} %get-tuple-element.94.g0), channel_id=1, source_target_pairs={{0,8},{4,12},{8,0},{12,4},{16,24},{20,28},{24,16},{28,20},{32,40},... | collective-permute-start | bytes 393224 | tf_op jit(solution)/shard_map/ppermute | solution.py:39
  136.2 6.3 %collective-permute-start.30 = (bf16[128,512]{1,0:T(8,128)(2,1)S(1)}, bf16[128,512]{1,0:T(8,128)(2,1)S(1)}, u32[]{:S(2)}, u32[]{:S(2)}) collective-permute-start(bf16[128,512]{1,0:T(8,128)(2,1)S(1)} %get-tuple-element.94.g0), channel_id=1, source_target_pairs={{0,4},{4,0},{8,12},{12,8},{16,20},{20,16},{24,28},{28,24},{32,36},... | collective-permute-start | bytes 393224 | tf_op jit(solution)/shard_map/ppermute | solution.py:39
  142.5 1.3 collective-permute-start.32
  144.3 10.7 %collective-permute-start.35 = (bf16[128,512]{1,0:T(8,128)(2,1)S(1)}, bf16[128,512]{1,0:T(8,128)(2,1)S(1)}, u32[]{:S(2)}, u32[]{:S(2)}) collective-permute-start(bf16[128,512]{1,0:T(8,128)(2,1)S(1)} %get-tuple-element.100), channel_id=1, source_target_pairs={{0,3},{1,0},{2,1},{3,2},{4,7},{5,4},{6,5},{7,6},{8,11},{9,8},{10,9... | collective-permute-start | bytes 393224 | tf_op jit(solution)/shard_map/ppermute | solution.py:17
  146.5 11.5 %collective-permute-start.34 = (bf16[128,512]{1,0:T(8,128)(2,1)S(1)}, bf16[128,512]{1,0:T(8,128)(2,1)S(1)}, u32[]{:S(2)}, u32[]{:S(2)}) collective-permute-start(bf16[128,512]{1,0:T(8,128)(2,1)S(1)} %get-tuple-element.98), channel_id=1, source_target_pairs={{0,1},{1,2},{2,3},{3,0},{4,5},{5,6},{6,7},{7,4},{8,9},{9,10},{10,1... | collective-permute-start | bytes 393224 | tf_op jit(solution)/shard_map/ppermute | solution.py:17
  146.5 11.5 %collective-permute-start.33 = (bf16[128,512]{1,0:T(8,128)(2,1)S(1)}, bf16[128,512]{1,0:T(8,128)(2,1)S(1)}, u32[]{:S(2)}, u32[]{:S(2)}) collective-permute-start(bf16[128,512]{1,0:T(8,128)(2,1)S(1)} %get-tuple-element.96), channel_id=1, source_target_pairs={{0,2},{1,3},{2,0},{3,1},{4,6},{5,7},{6,4},{7,5},{8,10},{9,11},{10,... | collective-permute-start | bytes 393224 | tf_op jit(solution)/shard_map/ppermute | solution.py:17
  148.0 12.2 %collective-permute-start.42 = (bf16[128,512]{1,0:T(8,128)(2,1)S(1)}, bf16[128,512]{1,0:T(8,128)(2,1)S(1)}, u32[]{:S(2)}, u32[]{:S(2)}) collective-permute-start(bf16[128,512]{1,0:T(8,128)(2,1)S(1)} %get-tuple-element.110), channel_id=1, source_target_pairs={{0,48},{4,52},{8,56},{12,60},{16,0},{20,4},{24,8},{28,12},{32,16},... | collective-permute-start | bytes 393224 | tf_op jit(solution)/shard_map/ppermute | solution.py:44
  154.1 14.7 %collective-permute-start.41 = (bf16[128,512]{1,0:T(8,128)(2,1)S(1)}, bf16[128,512]{1,0:T(8,128)(2,1)S(1)}, u32[]{:S(2)}, u32[]{:S(2)}) collective-permute-start(bf16[128,512]{1,0:T(8,128)(2,1)S(1)} %get-tuple-element.109), channel_id=1, source_target_pairs={{0,32},{4,36},{8,40},{12,44},{16,48},{20,52},{24,56},{28,60},{32,0... | collective-permute-start | bytes 393224 | tf_op jit(solution)/shard_map/ppermute | solution.py:44
  155.0 14.8 %collective-permute-start.40 = (bf16[128,512]{1,0:T(8,128)(2,1)S(1)}, bf16[128,512]{1,0:T(8,128)(2,1)S(1)}, u32[]{:S(2)}, u32[]{:S(2)}) collective-permute-start(bf16[128,512]{1,0:T(8,128)(2,1)S(1)} %get-tuple-element.108), channel_id=1, source_target_pairs={{0,16},{4,20},{8,24},{12,28},{16,32},{20,36},{24,40},{28,44},{32,4... | collective-permute-start | bytes 393224 | tf_op jit(solution)/shard_map/ppermute | solution.py:44
  (19 other events, 206.0 us)
Sparse Core Ops, SparseCore 0:
  9.8 41.4 all-gather.1
  100.6 61.1 reduce-scatter.1
